TPU v7x, 32 devices: a whole 2x2x4 slice. The times are simulated.
32 devices in a mesh: section: 1, ctx: 32 (over z, y, x, core).
Axes of the slice: x: 2, y: 2, z: 4, core: 2. Of those that a mesh axis runs over, the one named last changes fastest.
Arguments:
- hidden: bfloat16 [4096, 8192], P(('section', 'ctx')), may hold values from -12 to 12
- norm_gain: bfloat16 [8192], replicated, may hold values from 0.25 to 1.75
- w_qkv: bfloat16 [8192, 768], P('ctx'), may hold values from -2 to 2
- doc_ids: int32 [4096], P(('section', 'ctx')), may hold values from 0 to 31, never falling along the last dimension, each value on 1 to 1024 neighbouring positions
- target: int32 [4096], P(('section', 'ctx')), may hold values from 0 to 31, as said below
Outputs:
- attended: bfloat16 [4096, 512], P(('section', 'ctx'))
Inputs may be any that keep to these rules, and one draw needn't show every extreme that they name: Each device is the target of exactly 128 tokens; the tokens of one device with one target number 0, 4 or 8, and 8 occurs in every draw.
All inputs are finite; a program needn't handle non-finite values.
Results may differ from a plain program's by a relative error of at most 0.0078.
Values may be sent and summed in bfloat16 or wider, within the bound.
A program may use at most 64 MiB of HBM per device.

v0:
```python
import math

import jax
import jax.numpy as jnp
from jax import lax
from jax.sharding import PartitionSpec as P

HD = 128
QH = 4


def rotate(block, position):
    half = block.shape[-1] // 2
    freqs = 500000.0 ** (-(jnp.arange(half, dtype=jnp.float32) * 2.0) / block.shape[-1])
    angle = position.astype(jnp.float32)[:, None, None] * freqs[None, None, :]
    cosine = jnp.cos(angle)
    sine = jnp.sin(angle)
    first = block[..., :half]
    second = block[..., half:]
    return jnp.concatenate(
        [first * cosine - second * sine, second * cosine + first * sine], axis=-1
    )


def project(block, stream_idx, table, norm_gain, w_qkv):
    values_x = block.astype(jnp.float32)
    scale_norm = lax.rsqrt(jnp.mean(values_x * values_x, axis=1, keepdims=True) + 1e-05)
    normed = (values_x * scale_norm * norm_gain.astype(jnp.float32)).astype(jnp.bfloat16)
    proj = jnp.dot(
        normed, lax.all_gather(w_qkv, "ctx", axis=0, tiled=True), preferred_element_type=jnp.float32
    )
    own_doc = jnp.take(table, stream_idx)
    first_index = jnp.sum((table[None, :] < own_doc[:, None]).astype(jnp.int32), axis=1)
    position = stream_idx - first_index
    row_count = block.shape[0]
    query = rotate(proj[:, : QH * HD].reshape(row_count, QH, HD), position).reshape(
        row_count, QH * HD
    )
    key_rot = rotate(proj[:, QH * HD : (QH + 1) * HD].reshape(row_count, 1, HD), position).reshape(
        row_count, HD
    )
    return jnp.concatenate(
        [
            query.astype(jnp.bfloat16),
            key_rot.astype(jnp.bfloat16),
            proj[:, (QH + 1) * HD :].astype(jnp.bfloat16),
        ],
        axis=1,
    )


def pack(payload, dest_dev, stream_idx, n_dev, capacity):
    onehot = (dest_dev[:, None] == jnp.arange(n_dev, dtype=jnp.int32)[None, :]).astype(jnp.int32)
    ranking = jnp.sum(jnp.cumsum(onehot, axis=0) * onehot, axis=1) - 1
    slot_id = dest_dev * capacity + ranking
    buffer = jnp.zeros((n_dev * capacity, payload.shape[1]), payload.dtype).at[slot_id].set(payload)
    idx_buffer = jnp.full((n_dev * capacity,), -1, jnp.int32).at[slot_id].set(stream_idx)
    return (buffer.reshape(n_dev, capacity, payload.shape[1]), idx_buffer.reshape(n_dev, capacity))


def unpack(buffer, idx_buffer, row_count):
    flat = buffer.reshape(-1, buffer.shape[2])
    flat_idx = idx_buffer.reshape(-1)
    is_valid = flat_idx >= 0
    place = jnp.cumsum(is_valid.astype(jnp.int32)) - 1
    place = jnp.where(is_valid, place, row_count)
    rows_out = jnp.zeros((row_count, flat.shape[1]), flat.dtype).at[place].set(flat, mode="drop")
    idx_out = jnp.zeros((row_count,), jnp.int32).at[place].set(flat_idx, mode="drop")
    return (rows_out, idx_out)


def body(hidden, norm_gain, w_qkv, doc_ids, target):
    n_dev = lax.axis_size("ctx")
    row_count = hidden.shape[0]
    capacity = 2 * row_count // n_dev
    my_index = lax.axis_index("ctx")
    table = lax.all_gather(doc_ids, "ctx", axis=0, tiled=True)
    own_idx = my_index * row_count + jnp.arange(row_count, dtype=jnp.int32)
    buffer, idx_buffer = pack(hidden, target, own_idx, n_dev, capacity)
    moved_buf, moved_idx = (
        lax.all_to_all(buffer, "ctx", split_axis=0, concat_axis=0, tiled=True),
        lax.all_to_all(idx_buffer, "ctx", split_axis=0, concat_axis=0, tiled=True),
    )
    moved_rows, placed_idx = unpack(moved_buf, moved_idx, row_count)
    heads = project(moved_rows, placed_idx, table, norm_gain, w_qkv)
    query_rows = heads[:, : QH * HD].reshape(row_count * QH, HD)
    key_part = heads[:, QH * HD : (QH + 1) * HD]
    value_part = heads[:, (QH + 1) * HD :]
    query_idx = jnp.repeat(placed_idx, QH)
    query_doc = jnp.take(table, query_idx)
    inv_scale = 1.0 / math.sqrt(HD)
    start_carry = (
        jnp.full((row_count * QH,), -1e30, jnp.float32),
        jnp.zeros((row_count * QH,), jnp.float32),
        jnp.zeros((row_count * QH, HD), jnp.float32),
    )

    def attend_block(carry, block):
        running_max, running_sum, total_out = carry
        key_piece, value_piece, key_idx = block
        key_doc = jnp.take(table, key_idx)
        scores = (
            lax.dot_general(
                query_rows, key_piece, (((1,), (1,)), ((), ())), preferred_element_type=jnp.float32
            )
            * inv_scale
        )
        visible = (key_doc[None, :] == query_doc[:, None]) & (
            key_idx[None, :] <= query_idx[:, None]
        )
        new_max = jnp.maximum(running_max, jnp.max(jnp.where(visible, scores, -1e30), axis=1))
        weights = jnp.where(
            visible, jnp.exp(jnp.where(visible, scores, 0.0) - new_max[:, None]), 0.0
        )
        factor = jnp.exp(running_max - new_max)
        new_sum = running_sum * factor + jnp.sum(weights, axis=1)
        new_out = total_out * factor[:, None] + jnp.dot(
            weights.astype(jnp.bfloat16), value_piece, preferred_element_type=jnp.float32
        )
        return (new_max, new_sum, new_out)

    key_piece = lax.all_gather(key_part, "ctx", axis=0, tiled=True)
    value_piece = lax.all_gather(value_part, "ctx", axis=0, tiled=True)
    key_idx = lax.all_gather(placed_idx, "ctx", axis=0, tiled=True)
    key_count = key_piece.shape[0]
    width = math.gcd(key_count, 512)
    blocks = (
        key_piece.reshape(key_count // width, width, key_piece.shape[1]),
        value_piece.reshape(key_count // width, width, value_piece.shape[1]),
        key_idx.reshape(key_count // width, width),
    )

    def one_step(state, block):
        return (attend_block(state, block), None)

    state, unused = lax.scan(one_step, start_carry, blocks)
    final_max, final_sum, final_out = state
    result = (final_out / final_sum[:, None]).reshape(row_count, QH * HD)
    return result.astype(jnp.bfloat16)


def solution(mesh):
    in_specs = (
        P(("section", "ctx"), None),
        P(),
        P("ctx", None),
        P(("section", "ctx")),
        P(("section", "ctx")),
    )
    out_specs = P(("section", "ctx"), None)
    return jax.shard_map(body, mesh=mesh, in_specs=in_specs, out_specs=out_specs, check_vma=False)
```

profile of v0, /device:TPU:0, one launch (start us, length us, event | category | flops | bytes accessed | tf_op | source)
XLA Modules:
  0.0 379.2 jit_solution(3981121387013075090)
XLA Ops:
  6.5 0.7 all-gather.7.cloned.1.call-update
  7.3 0.7 fusion.32
  8.2 0.8 select_reduce_fusion.1
  9.0 0.7 compare_select_fusion.4
  9.7 1.0 scatter_custom_fusion
  10.7 0.7 all_to_all.9
  11.4 7.3 %all-to-all-start = ((s32[32,1,8]{2,1,0:T(1,128)}), s32[32,1,8]{2,1,0:T(1,128)S(1)}, u32[]{:S(2)}, u32[]{:S(2)}) async-start(s32[32,1,8]{2,1,0:T(1,128)} %bitcast), calls=%async_computation | async-start | bytes 32768 | tf_op jit(solution)/shard_map/all_to_all | solution.py:82
  18.7 7.0 %scatter_custom_fusion.2 = bf16[256,8192]{1,0:T(8,128)(2,1)} fusion(s32[128]{0:T(128)S(1)} %get-tuple-element.150, bf16[128,8192]{1,0:T(8,128)(2,1)} %param.9, bf16[]{:T(256)} %constant.42.clone.1), kind=kCustom, calls=%fused_computation.49 | custom fusion | bytes 4194816 | tf_op jit(solution)/shard_map/scatter | solution.py:56
  25.7 5.9 %all-to-all-start.1 = ((bf16[32,8,8192]{2,1,0:T(8,128)(2,1)}), bf16[32,8,8192]{2,1,0:T(8,128)(2,1)}, u32[]{:S(2)}, u32[]{:S(2)}) async-start(bf16[32,8,8192]{2,1,0:T(8,128)(2,1)} %bitcast.39), calls=%async_computation.1 | async-start | bytes 8388608 | tf_op jit(solution)/shard_map/all_to_all | solution.py:81
  31.7 141.4 %all-gather.2 = s32[32,1,128]{2,1,0:T(1,128)S(1)} all-gather(s32[1,1,128]{2,1,0:T(1,128)S(1)} %bitcast.52), channel_id=1, replica_groups=mesh['section'=1,'ctx'=32] {'ctx'}, dimensions={0}, use_global_device_ids=true | all-gather | bytes 16896 | tf_op jit(solution)/shard_map/all_gather | solution.py:77
  173.2 0.5 broadcast.260
  173.7 0.7 fusion.46
  174.5 0.3 reduce-window.9
  175.4 1.6 scatter_custom_fusion.1
  177.0 1.1 gather_fusion.1
  178.2 0.4 convert_reduce_fusion
  178.5 8.1 %scatter_custom_fusion.3 = bf16[128,8192]{1,0:T(8,128)(2,1)S(1)} fusion(s32[256]{0:T(256)S(1)} %bitcast.51, bf16[32,8,8192]{2,1,0:T(8,128)(2,1)} %all-to-all-done.1, bf16[]{:T(256)} %constant.42.clone.1), kind=kCustom, calls=%fused_computation.43 | custom fusion | bytes 6291458 | tf_op jit(solution)/shard_map/scatter | solution.py:67
  186.6 0.5 fusion.20
  187.2 6.5 %fusion.25 = f32[128,768]{1,0:T(8,128)S(1)} fusion(bf16[8192,768]{1,0:T(8,128)(2,1)} %all-gather.7.cloned.1.call-done, bf16[128,8192]{1,0:T(8,128)(2,1)S(1)} %scatter_custom_fusion.3, f32[8192]{0:T(1024)S(1)} %convert_element_type.49, f32[128]{0:T(128)S(1)} %add_rsqrt_fusion), kind=kOutput, calls=%fused_computation.45 | convolution fusion | flops 1614807040 | bytes 15106560 | tf_op jit(solution)/shard_map/dot_general | solution.py:29
  193.8 0.2 fusion.38
  194.0 0.6 pad_maximum_fusion.1
  194.7 0.6 slice.61
  195.7 3.1 gather_fusion.2
  198.8 63.5 %all-gather.1 = s32[32,1,128]{2,1,0:T(1,128)S(1)} all-gather(s32[1,1,128]{2,1,0:T(1,128)S(1)} %bitcast.48), channel_id=1, replica_groups=mesh['section'=1,'ctx'=32] {'ctx'}, dimensions={0}, use_global_device_ids=true | all-gather | bytes 16896 | tf_op jit(solution)/shard_map/all_gather | solution.py:124
  262.3 0.6 reduce.15
  263.0 0.3 multiply_cosine_fusion
  263.5 0.3 subtract_convert_fusion
  264.0 5.2 %all-gather.11.cloned.1.call-done = bf16[4096,1,128]{0,2,1:T(8,128)(2,1)} async-done(((bf16[128,1,128]{0,2,1:T(8,128)(2,1)}), bf16[4096,1,128]{0,2,1:T(8,128)(2,1)}) %all-gather.11.cloned.1.call-update) | async-done | bytes 1048592 | tf_op jit(solution)/shard_map/all_gather | solution.py:122
  269.2 1.6 copy.11
  270.8 54.4 %all-gather.9.cloned.1.call-done = bf16[4096,128]{1,0:T(8,128)(2,1)} async-done(((bf16[128,128]{1,0:T(8,128)(2,1)}), bf16[4096,128]{1,0:T(8,128)(2,1)}) %all-gather.9.cloned.1.call-update) | async-done | bytes 1048592 | tf_op jit(solution)/shard_map/all_gather | solution.py:123
  325.2 46.6 %while.15 = (s32[]{:T(128)}, f32[512]{0:T(512)S(1)}, f32[512]{0:T(512)S(1)}, f32[512,128]{1,0:T(8,128)S(1)}, s32[8,512]{1,0:T(8,128)S(1)}, /*index=5*/s32[4096]{...) while((s32[]{:T(128)}, f32[512]{0:T(512)S(1)}, ...), condition=%wide.region_13.15_spmd.clone, body=%wide.region_10.14_spmd.clone.sunk | while | flops 139665920 | bytes 4154513 | solution.py:136
  325.2 3.1 gather_fusion
  328.6 0.4 select_reduce_fusion.3
  329.0 0.4 fusion.57
  329.4 1.6 convolution_add_fusion.2
  331.1 3.1 gather_fusion
  334.4 0.4 select_reduce_fusion.3
  334.8 0.4 fusion.57
  335.2 1.6 convolution_add_fusion.2
  336.9 3.1 gather_fusion
  340.2 0.4 select_reduce_fusion.3
  340.7 0.4 fusion.57
  341.0 1.6 convolution_add_fusion.2
  342.7 3.1 gather_fusion
  346.1 0.4 select_reduce_fusion.3
  346.5 0.4 fusion.57
  346.9 1.6 convolution_add_fusion.2
  348.5 3.1 gather_fusion
  351.9 0.4 select_reduce_fusion.3
  352.3 0.4 fusion.57
  352.7 1.6 convolution_add_fusion.2
  354.4 3.1 gather_fusion
  357.7 0.4 select_reduce_fusion.3
  358.1 0.4 fusion.57
  358.5 1.6 convolution_add_fusion.2
  360.2 3.1 gather_fusion
  363.6 0.4 select_reduce_fusion.3
  364.0 0.4 fusion.57
  364.4 1.6 convolution_add_fusion.2
  366.0 3.1 gather_fusion
  369.4 0.4 select_reduce_fusion.3
  369.8 0.4 fusion.57
  370.2 1.6 convolution_add_fusion.2
  372.0 0.7 convert_element_type.56
  (116 shorter events, 3.8 us)
Async XLA Ops:
  6.5 180.6 %all-gather.7.cloned.1.call-start = ((), (), s32[]{:S(2)}) async-start(), calls=%async_computation.2 | async-start | bytes 12976128 | tf_op jit(solution)/shard_map/all_gather | solution.py:30
  11.4 14.4 %all-to-all-start = ((s32[32,1,8]{2,1,0:T(1,128)}), s32[32,1,8]{2,1,0:T(1,128)S(1)}, u32[]{:S(2)}, u32[]{:S(2)}) async-start(s32[32,1,8]{2,1,0:T(1,128)} %bitcast), calls=%async_computation | async-start | bytes 32768 | tf_op jit(solution)/shard_map/all_to_all | solution.py:82
  25.7 6.0 %copy-start = (bf16[8192]{0:T(1024)(128)(2,1)S(1)}, bf16[8192]{0:T(1024)(128)(2,1)}, u32[]{:S(2)}) copy-start(bf16[8192]{0:T(1024)(128)(2,1)} %param.10) | copy-start | bytes 49156
  25.7 6.0 %copy-start.1 = (s32[128]{0:T(128)S(1)}, s32[128]{0:T(128)}, u32[]{:S(2)}) copy-start(s32[128]{0:T(128)} %param.12) | copy-start | bytes 1540
  25.7 152.8 %all-to-all-start.1 = ((bf16[32,8,8192]{2,1,0:T(8,128)(2,1)}), bf16[32,8,8192]{2,1,0:T(8,128)(2,1)}, u32[]{:S(2)}, u32[]{:S(2)}) async-start(bf16[32,8,8192]{2,1,0:T(8,128)(2,1)} %bitcast.39), calls=%async_computation.1 | async-start | bytes 8388608 | tf_op jit(solution)/shard_map/all_to_all | solution.py:81
  31.6 237.5 %all-gather.11.cloned.1.call-start = ((), (), s32[]{:S(2)}) async-start(), calls=%async_computation.4 | async-start | bytes 1081344 | tf_op jit(solution)/shard_map/all_gather | solution.py:122
  194.7 130.5 %all-gather.9.cloned.1.call-start = ((), (), s32[]{:S(2)}) async-start(), calls=%async_computation.3 | async-start | bytes 1081344 | tf_op jit(solution)/shard_map/all_gather | solution.py:123
Sparse Core Ops, SparseCore 0:
  10.2 157.8 all-gather.6
  194.8 74.3 all-gather.10
  272.0 53.1 all-gather.8
where the time goes:
time: 380 us; the launch traced here: 379 us
  blocking collectives  205 us (54%)
  waiting for transfers between devices  60.5 us (16%)
  local copies, waits for them, and re-layouts  53.8 us (14%)
  matrix products  22.4 us (6%)
  between operations  13.4 us (4%)
  starting transfers between devices  13.3 us (4%)
  other arithmetic  10.2 us (3%)
    all_gather x1, blocking collectives, body(): table = lax.all_gather(doc_ids, 'ctx', axis=0, tiled=True)  141 us
    all_gather x1, blocking collectives, body(): key_idx = lax.all_gather(placed_idx, 'ctx', axis=0, tiled=True)  63.5 us
    all_gather x1, waiting for transfers between devices, body(): value_piece = lax.all_gather(value_part, 'ctx', axis=0, tiled=True)  54.4 us
    gather x8, local copies, waits for them, and re-layouts, attend_block(): key_doc = jnp.take(table, key_idx)  25.1 us
    dot_general x8, matrix products, attend_block(): jnp.dot(weights.astype(jnp.bfloat16), value_piece, preferred_element_type...  12.8 us
    scatter x1, local copies, waits for them, and re-layouts, unpack(): jnp.zeros((row_count, flat.shape[1]), flat.dtype).at[place]  8.09 us
  transfers between devices with their start and end apart: 5, of which 3 were waited for; matrix products, arithmetic and copies ran while one was open for 8% of the time, Pallas kernels for 0%

commit v1 on v0

v1 whole, which is shorter than its diff:
```python
import functools
import math

import jax
import jax.numpy as jnp
from jax import lax
from jax.experimental import pallas as pl
from jax.experimental.pallas import tpu as pltpu
from jax.sharding import PartitionSpec as P

HD = 128
QH = 4
MOST = 1024
NCH = 3
CW = 256
COLS = (2, 0, 1)
PLACE = (0, 2, 1, 3)
MESH = pl.DeviceIdType.MESH


def rotate(block, cosine, sine):
    return block * cosine + pltpu.roll(block, HD // 2, 1) * sine


def kernel(
    n_dev, hidden_ref, gain_ref, w_ref, doc_row_ref, doc_col_ref, tgt_row_ref, freq_ref, packed_ref,
    nsend, xg, wbuf, part, crecv, xsend, xrecv, kvbuf, dwin, bias, outbuf,
    h_send, h_recv, h_own, z_send, z_recv, y_send, y_recv, c_send, c_recv, x_send, x_recv,
    kv_send, kv_recv, d_send, d_recv,
):
    rows = hidden_ref.shape[0]
    depth = w_ref.shape[0]
    width = hidden_ref.shape[1]
    back = kvbuf.shape[0] - 1
    nz = n_dev // 8
    shards = n_dev // 4
    me = lax.axis_index("ctx")
    z, y, x, c = me // 8, (me // 4) % 2, (me // 2) % 2, me % 2
    spot = 2 * c + x
    shard = me // 4

    def remote(src, dst, send, recv, dev):
        return pltpu.make_async_remote_copy(
            src_ref=src, dst_ref=dst, send_sem=send, recv_sem=recv,
            device_id={"ctx": dev}, device_id_type=MESH,
        )

    dwin[...] = jnp.full_like(dwin, -1)
    kvbuf[...] = jnp.zeros_like(kvbuf)
    for n in range(NCH):
        wbuf[n, pl.ds(pl.multiple_of(shard * depth, depth), depth), :] = w_ref[
            :, COLS[n] * CW : (COLS[n] + 1) * CW
        ]
    dwin[back] = doc_row_ref[...]

    barrier = pltpu.get_barrier_semaphore()

    def greet(d, carry):
        pl.semaphore_signal(
            barrier, inc=1, device_id={"ctx": lax.rem(me + d, n_dev)}, device_id_type=MESH
        )
        return carry

    lax.fori_loop(1, n_dev, greet, 0)
    pl.semaphore_wait(barrier, n_dev - 1)

    y_dev = z * 8 + (1 - y) * 4 + x * 2 + c
    c_dev = z * 8 + y * 4 + x * 2 + (1 - c)
    x_dev = z * 8 + y * 4 + (1 - x) * 2 + c

    def slot(n, j):
        return wbuf.at[n, pl.ds(pl.multiple_of(j * depth, depth), depth), :]

    def y_copy(n, dz):
        j = lax.rem(z - dz + nz, nz) * 2 + y
        return remote(slot(n, j), slot(n, j), y_send.at[n, dz], y_recv.at[n, dz], y_dev)

    def z_copy(n, dz):
        dev = lax.rem(z + dz, nz) * 8 + y * 4 + x * 2 + c
        return remote(slot(n, shard), slot(n, shard), z_send.at[n, dz], z_recv.at[n, dz], dev)

    def d_copy(d):
        return remote(
            dwin.at[back], dwin.at[back - d], d_send.at[d - 1], d_recv.at[d - 1],
            lax.rem(me + d, n_dev),
        )

    def kv_copy(d):
        return remote(
            kvbuf.at[back], kvbuf.at[back - d], kv_send.at[d - 1], kv_recv.at[d - 1],
            lax.rem(me + d, n_dev),
        )

    def each_later(do):
        for d in range(1, back + 1):
            pl.when(me + d < n_dev)(functools.partial(do, d))

    def each_earlier(do):
        for d in range(1, back + 1):
            pl.when(me >= d)(functools.partial(do, d))

    each_later(lambda d: d_copy(d).start())
    for n in range(NCH):
        for dz in range(nz):
            if dz:
                z_copy(n, dz).start()
            else:
                y_copy(n, 0).start()

    step = 16

    def norm_rows(i, carry):
        at = pl.ds(pl.multiple_of(i * step, step), step)
        total = jnp.zeros((step, CW), jnp.float32)
        for b in range(width // CW):
            v = hidden_ref[at, b * CW : (b + 1) * CW].astype(jnp.float32)
            total = total + v * v
        scale = lax.rsqrt(jnp.sum(total, axis=1, keepdims=True) * (1.0 / width) + 1e-05)
        for b in range(width // depth):
            v = hidden_ref[at, b * depth : (b + 1) * depth].astype(jnp.float32)
            g = gain_ref[:, b * depth : (b + 1) * depth]
            nsend[PLACE[b % 4], at, (b // 4) * depth : (b // 4 + 1) * depth] = (
                v * scale * g
            ).astype(jnp.bfloat16)
        return carry

    lax.fori_loop(0, rows // step, norm_rows, 0)

    def h_copy(k):
        dx, dc = ((1, 0), (1, 1), (0, 1))[k]
        ox = 1 - x if dx else x
        oc = 1 - c if dc else c
        return remote(
            nsend.at[2 * oc + ox], xg.at[spot], h_send.at[k], h_recv.at[k],
            z * 8 + y * 4 + ox * 2 + oc,
        )

    for k in range(3):
        h_copy(k).start()
    own = pltpu.make_async_copy(nsend.at[spot], xg.at[spot], h_own)
    own.start()

    def forward(n):
        for dz in range(1, nz):
            z_copy(n, dz).wait_recv()
            y_copy(n, dz).start()

    each_earlier(lambda d: d_copy(d).wait_recv())
    count = jnp.zeros((rows, 1), jnp.float32)
    for s in range(back + 1):
        seen = doc_col_ref[...] == dwin[s, 0:1, :]
        if s == back:
            seen = seen & (
                lax.broadcasted_iota(jnp.int32, (rows, rows), 1)
                <= lax.broadcasted_iota(jnp.int32, (rows, rows), 0)
            )
        bias[:, s * rows : (s + 1) * rows] = jnp.where(seen, 0.0, -1e30)
        count = count + jnp.sum(jnp.where(seen, 1.0, 0.0), axis=1, keepdims=True)
    angle = (count - 1.0) * freq_ref[...]
    cosine = jnp.cos(angle)
    sine = jnp.sin(angle) * jnp.where(
        lax.broadcasted_iota(jnp.int32, (rows, HD), 1) < HD // 2, -1.0, 1.0
    )

    def matmul(n):
        for dz in range(nz):
            y_copy(n, dz).wait_recv()
        left = xg[...].reshape(4 * rows, xg.shape[2])
        part[n] = jnp.dot(left, wbuf[n], preferred_element_type=jnp.float32).reshape(
            2, 2, rows, CW
        )

    def c_copy(n):
        return remote(part.at[n, 1 - c], crecv.at[n], c_send.at[n], c_recv.at[n], c_dev)

    def x_copy(n):
        return remote(xsend.at[n], xrecv.at[n], x_send.at[n], x_recv.at[n], x_dev)

    def cross(n):
        c_copy(n).wait_recv()
        xsend[n] = part[n, c, 1 - x] + crecv[n, 1 - x]
        x_copy(n).start()

    def finish(n):
        x_copy(n).wait_recv()
        return part[n, c, x] + crecv[n, x] + xrecv[n]

    def attend(head, query):
        keys = kvbuf[:, :, :HD].reshape((back + 1) * rows, HD)
        values = kvbuf[:, :, HD:].reshape((back + 1) * rows, HD)
        scores = (
            lax.dot_general(
                query, keys, (((1,), (1,)), ((), ())), preferred_element_type=jnp.float32
            )
            * (1.0 / math.sqrt(HD))
            + bias[...]
        )
        weights = jnp.exp(scores - jnp.max(scores, axis=1, keepdims=True))
        total = jnp.sum(weights, axis=1, keepdims=True)
        out = jnp.dot(weights.astype(jnp.bfloat16), values, preferred_element_type=jnp.float32)
        outbuf[:, head * HD : (head + 1) * HD] = (out / total).astype(jnp.bfloat16)

    forward(0)
    forward(1)
    own.wait()
    for k in range(3):
        h_copy(k).wait_recv()
    matmul(0)
    c_copy(0).start()
    matmul(1)
    c_copy(1).start()
    cross(0)
    cross(1)
    forward(2)
    kv = finish(0)
    kvbuf[back, :, :HD] = rotate(kv[:, :HD], cosine, sine).astype(jnp.bfloat16)
    kvbuf[back, :, HD:] = kv[:, HD:].astype(jnp.bfloat16)
    each_later(lambda d: kv_copy(d).start())
    matmul(2)
    c_copy(2).start()
    heads = finish(1)
    cross(2)
    each_earlier(lambda d: kv_copy(d).wait_recv())
    for h in range(2):
        attend(h, rotate(heads[:, h * HD : (h + 1) * HD], cosine, sine).astype(jnp.bfloat16))
    heads = finish(2)
    for h in range(2):
        attend(h + 2, rotate(heads[:, h * HD : (h + 1) * HD], cosine, sine).astype(jnp.bfloat16))

    tgt = tgt_row_ref[0:1, :]
    tgt_mat = jnp.transpose(jnp.broadcast_to(tgt, (rows, rows)))
    earlier = (tgt_mat == tgt) & (
        lax.broadcasted_iota(jnp.int32, (rows, rows), 0)
        < lax.broadcasted_iota(jnp.int32, (rows, rows), 1)
    )
    rank = jnp.sum(jnp.where(earlier, 1.0, 0.0), axis=0, keepdims=True).astype(jnp.int32)
    cap = packed_ref.shape[0] // n_dev
    place = tgt * cap + rank
    pick = jnp.where(
        lax.broadcasted_iota(jnp.int32, (packed_ref.shape[0], rows), 0) == place, 1.0, 0.0
    ).astype(jnp.bfloat16)
    packed_ref[...] = jnp.dot(pick, outbuf[...], preferred_element_type=jnp.float32).astype(
        jnp.bfloat16
    )

    each_later(lambda d: d_copy(d).wait_send())
    each_later(lambda d: kv_copy(d).wait_send())
    for k in range(3):
        h_copy(k).wait_send()
    for n in range(NCH):
        for dz in range(nz):
            if dz:
                z_copy(n, dz).wait_send()
            y_copy(n, dz).wait_send()
        c_copy(n).wait_send()
        x_copy(n).wait_send()


def body(hidden, norm_gain, w_qkv, doc_ids, target):
    n_dev = lax.axis_size("ctx")
    rows, width = hidden.shape
    depth = w_qkv.shape[0]
    cap = 2 * rows // n_dev
    back = -(-(MOST - 1) // rows)
    nz = n_dev // 8
    me = lax.axis_index("ctx")
    half = HD // 2
    freqs = 500000.0 ** (-(jnp.arange(half, dtype=jnp.float32) * 2.0) / HD)
    freq_row = jnp.concatenate([freqs, freqs])[None, :]
    doc_row = jnp.broadcast_to(doc_ids[None, :], (8, rows))
    tgt_row = jnp.broadcast_to(target[None, :], (8, rows))
    bf16, f32 = jnp.bfloat16, jnp.float32
    dma = pltpu.SemaphoreType.DMA
    packed = pl.pallas_call(
        functools.partial(kernel, n_dev),
        out_shape=jax.ShapeDtypeStruct((n_dev * cap, QH * HD), bf16),
        in_specs=[pl.BlockSpec(memory_space=pltpu.VMEM)] * 7,
        out_specs=pl.BlockSpec(memory_space=pltpu.VMEM),
        scratch_shapes=[
            pltpu.VMEM((4, rows, width // 4), bf16),
            pltpu.VMEM((4, rows, width // 4), bf16),
            pltpu.VMEM((NCH, width // 4, CW), bf16),
            pltpu.VMEM((NCH, 2, 2, rows, CW), f32),
            pltpu.VMEM((NCH, 2, rows, CW), f32),
            pltpu.VMEM((NCH, rows, CW), f32),
            pltpu.VMEM((NCH, rows, CW), f32),
            pltpu.VMEM((back + 1, rows, 2 * HD), bf16),
            pltpu.VMEM((back + 1, 8, rows), jnp.int32),
            pltpu.VMEM((rows, (back + 1) * rows), f32),
            pltpu.VMEM((rows, QH * HD), bf16),
            dma((3,)), dma((3,)), dma,
            dma((NCH, nz)), dma((NCH, nz)), dma((NCH, nz)), dma((NCH, nz)),
            dma((NCH,)), dma((NCH,)), dma((NCH,)), dma((NCH,)),
            dma((back,)), dma((back,)), dma((back,)), dma((back,)),
        ],
        compiler_params=pltpu.CompilerParams(
            collective_id=0, has_side_effects=True, vmem_limit_bytes=48 * 1024 * 1024
        ),
        cost_estimate=pl.CostEstimate(
            flops=2 * rows * width * 768, bytes_accessed=4 * 1024 * 1024, transcendentals=0
        ),
    )(
        hidden, norm_gain.astype(f32)[None, :], w_qkv, doc_row, doc_ids[:, None], tgt_row, freq_row
    )
    table = lax.all_gather(target, "ctx", axis=0, tiled=False)
    moved = lax.all_to_all(
        packed.reshape(n_dev, cap, QH * HD), "ctx", split_axis=0, concat_axis=0, tiled=True
    )
    counts = jnp.sum((table == me).astype(jnp.int32), axis=1)
    first = jnp.cumsum(counts) - counts
    lane = jnp.arange(cap, dtype=jnp.int32)[None, :]
    dest = jnp.where(lane < counts[:, None], first[:, None] + lane, -1).reshape(-1)
    pick = (jnp.arange(rows, dtype=jnp.int32)[:, None] == dest[None, :]).astype(bf16)
    return jnp.dot(pick, moved.reshape(n_dev * cap, QH * HD), preferred_element_type=f32).astype(bf16)


def solution(mesh):
    in_specs = (
        P(("section", "ctx"), None),
        P(),
        P("ctx", None),
        P(("section", "ctx")),
        P(("section", "ctx")),
    )
    out_specs = P(("section", "ctx"), None)
    return jax.shard_map(body, mesh=mesh, in_specs=in_specs, out_specs=out_specs, check_vma=False)
```

time: 380 us -> 125 us (0.33)
  blocking collectives: 205 us -> 41.6 us
  Pallas kernels: 0 us -> 63.4 us
  waiting for transfers between devices: 60.5 us -> 0.01 us
  local copies, waits for them, and re-layouts: 53.8 us -> 4.85 us
  matrix products: 22.4 us -> 0.85 us
  between operations: 13.4 us -> 0.06 us
  other arithmetic: 10.2 us -> 1.72 us
    all_gather x2 -> x1, blocking collectives: 205 us -> 41.6 us  [body(): table = lax.all_gather(target, 'ctx', axis=0, tiled=False)]
    pallas_call x0 -> x1, Pallas kernels: none -> 63.4 us  [body(): pl.pallas_call(functools.partial(kernel, n_dev), out_shape=jax.ShapeDtype...]
    all_gather x3 -> x0, waiting for transfers between devices: 59.6 us -> none  [the longest x1 54.4 us: body(): value_piece = lax.all_gather(value_part, 'ctx', axis=0, tiled=True)]
    gather x10 -> x0, local copies, waits for them, and re-layouts: 29.4 us -> none  [the longest x8 25.1 us: attend_block(): key_doc = jnp.take(table, key_idx)]
    dot_general x17 -> x1, matrix products: 22.4 us -> 0.85 us  [body(): jnp.dot(pick, moved.reshape(n_dev * cap, QH * HD), preferred_element_type...]
    scatter x4 -> x0, local copies, waits for them, and re-layouts: 17.7 us -> none  [the longest x1 8.09 us: unpack(): jnp.zeros((row_count, flat.shape[1]), flat.dtype).at[place]]
    reduce_sum x11 -> x1, other arithmetic: 4.63 us -> 0.66 us  [body(): counts = jnp.sum((table == me).astype(jnp.int32), axis=1)]
    all_to_all x2 -> x1, starting transfers between devices: 13.2 us -> 12.4 us  [body(): lax.all_to_all(packed.reshape(n_dev, cap, QH * HD), 'ctx', split_axis=0,...]
  transfers between devices with their start and end apart: 5 -> 1, of which waited for: 3 -> 0; matrix products, arithmetic and copies ran while one was open for 8% -> 1% of each run, Pallas kernels for 0% -> 0%
where the time goes in v1:
time: 125 us
  Pallas kernels  63.4 us (51%)
  blocking collectives  41.6 us (33%)
  starting transfers between devices  12.4 us (10%)
  local copies, waits for them, and re-layouts  4.85 us (4%)
  other arithmetic  1.72 us (1%)
    pallas_call x1, Pallas kernels, body(): pl.pallas_call(functools.partial(kernel, n_dev), out_shape=jax.ShapeDtype...  63.4 us
    all_gather x1, blocking collectives, body(): table = lax.all_gather(target, 'ctx', axis=0, tiled=False)  41.6 us
    all_to_all x1, starting transfers between devices, body(): lax.all_to_all(packed.reshape(n_dev, cap, QH * HD), 'ctx', split_axis=0,...  12.4 us
    unnamed x6, local copies, waits for them, and re-layouts  2.59 us
  transfers between devices with their start and end apart: 1, of which 0 were waited for; matrix products, arithmetic and copies ran while one was open for 1% of the time, Pallas kernels for 0%

profile of v1, /device:TPU:0, one launch (start us, length us, event | category | flops | bytes accessed | tf_op | source)
XLA Modules:
  0.0 124.8 jit_solution(7982826886633435397)
XLA Ops:
  0.0 0.7 broadcast_in_dim.38
  0.7 0.8 copy.11.doc_col_ref
  1.5 0.1 maximum_bitcast_fusion.freq_ref
  1.6 0.7 broadcast_in_dim.34.doc_row_ref
  2.2 0.7 broadcast_in_dim.36.tgt_row_ref
  2.9 0.0 copy-start
  2.9 1.6 %copy-done = bf16[128,8192]{1,0:T(8,128)(2,1)S(1)} copy-done((bf16[128,8192]{1,0:T(8,128)(2,1)S(1)}, bf16[128,8192]{1,0:T(8,128)(2,1)}, u32[]{:S(2)}) %copy-start) | copy-done | bytes 2097176
  4.5 0.0 copy-start.1
  4.5 1.0 copy-done.1
  5.5 0.0 copy-start.2
  5.5 63.4 %shard_map.55 = bf16[256,512]{1,0:T(8,128)(2,1)} custom-call(bf16[128,8192]{1,0:T(8,128)(2,1)S(1)} %copy-done, f32[1,8192]{1,0:T(1,128)S(1)} %bitcast.10, bf16[256,768]{1,0:T(8,128)(2,1)S(1)} %copy-done.1, s32[8,128]{1,0:T(8,128)S(1)} %broadcast_in_dim.34.doc_row_ref, s32[128,1]{1,0:T(8,128)S(1)} %copy.11.doc_col_ref, ...), custom_call_target="tpu_custom_call" | custom-call | flops 1610612736 | bytes 4194304 | tf_op jit(solution)/shard_map/pallas_call | solution.py:274
  68.9 12.4 %all-to-all-start = ((bf16[32,8,512]{2,1,0:T(8,128)(2,1)}), bf16[32,8,512]{2,1,0:T(8,128)(2,1)S(1)}, u32[]{:S(2)}, u32[]{:S(2)}) async-start(bf16[32,8,512]{2,1,0:T(8,128)(2,1)} %bitcast.5), calls=%async_computation | async-start | bytes 524288 | tf_op jit(solution)/shard_map/all_to_all | solution.py:306
  81.3 0.0 copy-done.2
  81.3 41.6 %all-gather.1 = s32[32,1,128]{2,1,0:T(1,128)S(1)} all-gather(s32[1,1,128]{2,1,0:T(1,128)S(1)} %bitcast.13), channel_id=2, replica_groups=mesh['section'=1,'ctx'=32] {'ctx'}, dimensions={0}, use_global_device_ids=true | all-gather | bytes 16896 | tf_op jit(solution)/shard_map/all_gather | solution.py:305
  122.9 0.7 fusion.2
  123.5 0.1 copy.10
  123.6 0.1 reduce-window.8
  123.7 0.1 reduce.1
  123.8 0.1 add_select_fusion
  123.9 0.1 select_n.12
  124.0 0.0 all-to-all-done
  124.0 0.9 convolution_convert_fusion
  (2 shorter events, 0.0 us)
Async XLA Ops:
  2.9 1.6 %copy-start = (bf16[128,8192]{1,0:T(8,128)(2,1)S(1)}, bf16[128,8192]{1,0:T(8,128)(2,1)}, u32[]{:S(2)}) copy-start(bf16[128,8192]{1,0:T(8,128)(2,1)} %hidden_ref.1) | copy-start | bytes 6291460
  4.5 1.0 copy-start.1
  5.5 75.8 %copy-start.2 = (s32[128]{0:T(128)S(1)}, s32[128]{0:T(128)}, u32[]{:S(2)}) copy-start(s32[128]{0:T(128)} %param.9) | copy-start | bytes 1540
  68.9 55.1 %all-to-all-start = ((bf16[32,8,512]{2,1,0:T(8,128)(2,1)}), bf16[32,8,512]{2,1,0:T(8,128)(2,1)S(1)}, u32[]{:S(2)}, u32[]{:S(2)}) async-start(bf16[32,8,512]{2,1,0:T(8,128)(2,1)} %bitcast.5), calls=%async_computation | async-start | bytes 524288 | tf_op jit(solution)/shard_map/all_to_all | solution.py:306

commit v2 on v1

v2 whole, which is shorter than its diff:
```python
import functools
import math

import jax
import jax.numpy as jnp
import numpy as np
from jax import lax
from jax.experimental import pallas as pl
from jax.experimental.pallas import tpu as pltpu
from jax.sharding import PartitionSpec as P

HD = 128
QH = 4
MOST = 1024
NCH = 3
CW = 256
COLS = (2, 0, 1)
PLACE = (0, 2, 1, 3)
MESH = pl.DeviceIdType.MESH


def rotate(block, cosine, sine):
    return block * cosine + pltpu.roll(block, HD // 2, 1) * sine


def kernel(
    n_dev, hidden_hbm, gain_ref, w_hbm, doc_ref, tgt_ref, freq_ref, result_ref,
    hidden_ref, gain32, nsend, xg, wbuf, part, crecv, xsend, xrecv, kvbuf, ids, bias, outbuf, abuf, rbuf,
    load_sem, w_sem,
    h_send, h_recv, h_own, z_send, z_recv, y_send, y_recv, c_send, c_recv, x_send, x_recv,
    kv_send, kv_recv, i_send, i_recv, a_send, a_recv,
):
    rows = hidden_ref.shape[0]
    depth = w_hbm.shape[0]
    width = hidden_ref.shape[1]
    back = kvbuf.shape[0] - 1
    nz = n_dev // 8
    shards = n_dev // 4
    me = lax.axis_index("ctx")
    z, y, x, c = me // 8, (me // 4) % 2, (me // 2) % 2, me % 2
    spot = 2 * c + x
    shard = me // 4

    def remote(src, dst, send, recv, dev):
        return pltpu.make_async_remote_copy(
            src_ref=src, dst_ref=dst, send_sem=send, recv_sem=recv,
            device_id={"ctx": dev}, device_id_type=MESH,
        )

    def slot(n, j):
        return wbuf.at[n, pl.ds(pl.multiple_of(j * depth, depth), depth), :]

    def w_load(n):
        return pltpu.make_async_copy(
            w_hbm.at[:, COLS[n] * CW : (COLS[n] + 1) * CW], slot(n, shard), w_sem.at[n]
        )

    for n in range(NCH):
        w_load(n).start()
    load = pltpu.make_async_copy(hidden_hbm, hidden_ref, load_sem)
    load.start()
    doc = doc_ref[...]
    tgt = tgt_ref[...]
    ids[me] = jnp.where(
        lax.broadcasted_iota(jnp.int32, (8, rows), 0) == 0,
        jnp.broadcast_to(doc, (8, rows)),
        jnp.broadcast_to(tgt, (8, rows)),
    )

    barrier = pltpu.get_barrier_semaphore()

    def greet(d, carry):
        pl.semaphore_signal(
            barrier, inc=1, device_id={"ctx": lax.rem(me + d, n_dev)}, device_id_type=MESH
        )
        return carry

    lax.fori_loop(1, n_dev, greet, 0)
    gain32[...] = gain_ref[...].astype(jnp.float32)
    kvbuf[...] = jnp.zeros_like(kvbuf)
    pl.semaphore_wait(barrier, n_dev - 1)

    y_dev = z * 8 + (1 - y) * 4 + x * 2 + c
    c_dev = z * 8 + y * 4 + x * 2 + (1 - c)
    x_dev = z * 8 + y * 4 + (1 - x) * 2 + c

    def y_copy(n, dz):
        j = lax.rem(z - dz + nz, nz) * 2 + y
        return remote(slot(n, j), slot(n, j), y_send.at[n, dz], y_recv.at[n, dz], y_dev)

    def z_copy(n, dz):
        dev = lax.rem(z + dz, nz) * 8 + y * 4 + x * 2 + c
        return remote(slot(n, shard), slot(n, shard), z_send.at[n, dz], z_recv.at[n, dz], dev)

    def i_copy(d):
        return remote(ids.at[me], ids.at[me], i_send.at[d], i_recv.at[d], lax.rem(me + d, n_dev))

    def a_copy(d):
        dev = lax.rem(me + d, n_dev)
        return remote(abuf.at[dev], rbuf.at[me], a_send.at[d], a_recv.at[d], dev)

    def each_other(do):
        def one(d, carry):
            do(d)
            return carry

        lax.fori_loop(1, n_dev, one, 0)

    def kv_copy(d):
        return remote(
            kvbuf.at[back], kvbuf.at[back - d], kv_send.at[d - 1], kv_recv.at[d - 1],
            lax.rem(me + d, n_dev),
        )

    def each_later(do):
        for d in range(1, back + 1):
            pl.when(me + d < n_dev)(functools.partial(do, d))

    def each_earlier(do):
        for d in range(1, back + 1):
            pl.when(me >= d)(functools.partial(do, d))

    for n in range(NCH):
        w_load(n).wait()
        for dz in range(nz):
            if dz:
                z_copy(n, dz).start()
            else:
                y_copy(n, 0).start()
        if n == 0:
            each_other(lambda d: i_copy(d).start())
    load.wait()

    step = 16

    def norm_rows(i, carry):
        at = pl.ds(pl.multiple_of(i * step, step), step)
        total = jnp.zeros((step, CW), jnp.float32)
        for b in range(width // CW):
            v = hidden_ref[at, b * CW : (b + 1) * CW].astype(jnp.float32)
            total = total + v * v
        scale = lax.rsqrt(jnp.sum(total, axis=1, keepdims=True) * (1.0 / width) + 1e-05)
        for b in range(width // depth):
            v = hidden_ref[at, b * depth : (b + 1) * depth].astype(jnp.float32)
            g = gain32[:, b * depth : (b + 1) * depth]
            nsend[PLACE[b % 4], at, (b // 4) * depth : (b // 4 + 1) * depth] = (
                v * scale * g
            ).astype(jnp.bfloat16)
        return carry

    lax.fori_loop(0, rows // step, norm_rows, 0)

    def h_copy(k):
        dx, dc = ((1, 0), (1, 1), (0, 1))[k]
        ox = 1 - x if dx else x
        oc = 1 - c if dc else c
        return remote(
            nsend.at[2 * oc + ox], xg.at[spot], h_send.at[k], h_recv.at[k],
            z * 8 + y * 4 + ox * 2 + oc,
        )

    for k in range(3):
        h_copy(k).start()
    own = pltpu.make_async_copy(nsend.at[spot], xg.at[spot], h_own)
    own.start()

    def forward(n):
        for dz in range(1, nz):
            z_copy(n, dz).wait_recv()
            y_copy(n, dz).start()

    def matmul(n):
        for dz in range(nz):
            y_copy(n, dz).wait_recv()
        left = xg[...].reshape(4 * rows, xg.shape[2])
        part[n] = jnp.dot(left, wbuf[n], preferred_element_type=jnp.float32).reshape(
            2, 2, rows, CW
        )

    def c_copy(n):
        return remote(part.at[n, 1 - c], crecv.at[n], c_send.at[n], c_recv.at[n], c_dev)

    def x_copy(n):
        return remote(xsend.at[n], xrecv.at[n], x_send.at[n], x_recv.at[n], x_dev)

    def cross(n):
        c_copy(n).wait_recv()
        xsend[n] = part[n, c, 1 - x] + crecv[n, 1 - x]
        x_copy(n).start()

    def finish(n):
        x_copy(n).wait_recv()
        return part[n, c, x] + crecv[n, x] + xrecv[n]

    def attend(head, query):
        keys = kvbuf[:, :, :HD].reshape((back + 1) * rows, HD)
        values = kvbuf[:, :, HD:].reshape((back + 1) * rows, HD)
        scores = (
            lax.dot_general(
                query, keys, (((1,), (1,)), ((), ())), preferred_element_type=jnp.float32
            )
            * (1.0 / math.sqrt(HD))
            + bias[...]
        )
        weights = jnp.exp(scores - jnp.max(scores, axis=1, keepdims=True))
        total = jnp.sum(weights, axis=1, keepdims=True)
        out = jnp.dot(weights.astype(jnp.bfloat16), values, preferred_element_type=jnp.float32)
        outbuf[:, head * HD : (head + 1) * HD] = (out / total).astype(jnp.bfloat16)

    forward(0)
    each_other(lambda d: i_copy(d).wait_recv())
    doc_col = jnp.transpose(jnp.broadcast_to(doc, (rows, rows)))
    count = jnp.zeros((rows, 1), jnp.float32)
    for s in range(back + 1):
        near = ids[lax.rem(me + n_dev - back + s, n_dev), 0:1, :]
        seen = doc_col == jnp.where(me + s >= back, near, -1)
        if s == back:
            seen = seen & (
                lax.broadcasted_iota(jnp.int32, (rows, rows), 1)
                <= lax.broadcasted_iota(jnp.int32, (rows, rows), 0)
            )
        bias[:, s * rows : (s + 1) * rows] = jnp.where(seen, 0.0, -1e30)
        count = count + jnp.sum(jnp.where(seen, 1.0, 0.0), axis=1, keepdims=True)
    angle = (count - 1.0) * freq_ref[...]
    cosine = jnp.cos(angle)
    sine = jnp.sin(angle) * jnp.where(
        lax.broadcasted_iota(jnp.int32, (rows, HD), 1) < HD // 2, -1.0, 1.0
    )

    forward(1)
    own.wait()
    for k in range(3):
        h_copy(k).wait_recv()
    matmul(0)
    c_copy(0).start()
    matmul(1)
    c_copy(1).start()
    cross(0)
    cross(1)
    forward(2)
    kv = finish(0)
    kvbuf[back, :, :HD] = rotate(kv[:, :HD], cosine, sine).astype(jnp.bfloat16)
    kvbuf[back, :, HD:] = kv[:, HD:].astype(jnp.bfloat16)
    each_later(lambda d: kv_copy(d).start())
    matmul(2)
    c_copy(2).start()
    heads = finish(1)
    cross(2)
    each_earlier(lambda d: kv_copy(d).wait_recv())
    for h in range(2):
        attend(h, rotate(heads[:, h * HD : (h + 1) * HD], cosine, sine).astype(jnp.bfloat16))
    heads = finish(2)
    for h in range(2):
        attend(h + 2, rotate(heads[:, h * HD : (h + 1) * HD], cosine, sine).astype(jnp.bfloat16))

    tgt_mat = jnp.transpose(jnp.broadcast_to(tgt, (rows, rows)))
    earlier = (tgt_mat == tgt) & (
        lax.broadcasted_iota(jnp.int32, (rows, rows), 0)
        < lax.broadcasted_iota(jnp.int32, (rows, rows), 1)
    )
    rank = jnp.sum(jnp.where(earlier, 1.0, 0.0), axis=0, keepdims=True).astype(jnp.int32)
    cap = abuf.shape[1] // 2
    slots = n_dev * 2 * cap
    slot_col = lax.broadcasted_iota(jnp.int32, (slots, rows), 0)
    place = tgt * (2 * cap) + rank
    half = QH * HD // 2
    packed = jnp.dot(
        jnp.where(slot_col == place, 1.0, 0.0).astype(jnp.bfloat16),
        outbuf[:, :half],
        preferred_element_type=jnp.float32,
    ) + jnp.dot(
        jnp.where(slot_col == place + cap, 1.0, 0.0).astype(jnp.bfloat16),
        outbuf[:, half:],
        preferred_element_type=jnp.float32,
    )
    abuf[...] = packed.astype(jnp.bfloat16).reshape(abuf.shape)
    each_other(lambda d: a_copy(d).start())
    rbuf[me] = abuf[me]

    counts = jnp.sum(jnp.where(ids[:, 1, :] == me, 1.0, 0.0), axis=1, keepdims=True)
    lane = lax.broadcasted_iota(jnp.int32, (n_dev, slots), 1)
    source = lax.broadcasted_iota(jnp.int32, (n_dev, slots), 0)
    owner = lane // (2 * cap)
    count_row = jnp.sum(jnp.where(source == owner, counts, 0.0), axis=0, keepdims=True)
    first_row = jnp.sum(jnp.where(source < owner, counts, 0.0), axis=0, keepdims=True)
    inner = lax.broadcasted_iota(jnp.int32, (1, slots), 1) % (2 * cap)
    index = inner % cap
    goal = jnp.where(
        index < count_row.astype(jnp.int32), first_row.astype(jnp.int32) + index, -1
    )
    out_row = lax.broadcasted_iota(jnp.int32, (rows, slots), 0)
    picks = [
        jnp.where(out_row == jnp.where(inner // cap == h, goal, -1), 1.0, 0.0).astype(jnp.bfloat16)
        for h in range(2)
    ]
    each_other(lambda d: a_copy(d).wait_recv())
    arrived = rbuf[...].reshape(slots, half)
    for h in range(2):
        result_ref[:, h * half : (h + 1) * half] = jnp.dot(
            picks[h], arrived, preferred_element_type=jnp.float32
        ).astype(jnp.bfloat16)

    each_other(lambda d: i_copy(d).wait_send())
    each_other(lambda d: a_copy(d).wait_send())
    each_later(lambda d: kv_copy(d).wait_send())
    for k in range(3):
        h_copy(k).wait_send()
    for n in range(NCH):
        for dz in range(nz):
            if dz:
                z_copy(n, dz).wait_send()
            y_copy(n, dz).wait_send()
        c_copy(n).wait_send()
        x_copy(n).wait_send()


def body(hidden, norm_gain, w_qkv, doc_ids, target):
    n_dev = lax.axis_size("ctx")
    rows, width = hidden.shape
    depth = w_qkv.shape[0]
    cap = 2 * rows // n_dev
    back = -(-(MOST - 1) // rows)
    nz = n_dev // 8
    freqs = 500000.0 ** (-(np.arange(HD // 2, dtype=np.float64) * 2.0) / HD)
    freq_row = jnp.asarray(np.concatenate([freqs, freqs])[None, :], jnp.float32)
    bf16, f32 = jnp.bfloat16, jnp.float32
    dma = pltpu.SemaphoreType.DMA
    return pl.pallas_call(
        functools.partial(kernel, n_dev),
        out_shape=jax.ShapeDtypeStruct((rows, QH * HD), bf16),
        in_specs=[
            pl.BlockSpec(memory_space=pltpu.HBM if i in (0, 2) else pltpu.VMEM) for i in range(6)
        ],
        out_specs=pl.BlockSpec(memory_space=pltpu.VMEM),
        scratch_shapes=[
            pltpu.VMEM((rows, width), bf16),
            pltpu.VMEM((1, width), f32),
            pltpu.VMEM((4, rows, width // 4), bf16),
            pltpu.VMEM((4, rows, width // 4), bf16),
            pltpu.VMEM((NCH, width // 4, CW), bf16),
            pltpu.VMEM((NCH, 2, 2, rows, CW), f32),
            pltpu.VMEM((NCH, 2, rows, CW), f32),
            pltpu.VMEM((NCH, rows, CW), f32),
            pltpu.VMEM((NCH, rows, CW), f32),
            pltpu.VMEM((back + 1, rows, 2 * HD), bf16),
            pltpu.VMEM((n_dev, 8, rows), jnp.int32),
            pltpu.VMEM((rows, (back + 1) * rows), f32),
            pltpu.VMEM((rows, QH * HD), bf16),
            pltpu.VMEM((n_dev, 2 * cap, QH * HD // 2), bf16),
            pltpu.VMEM((n_dev, 2 * cap, QH * HD // 2), bf16),
            dma, dma((NCH,)),
            dma((3,)), dma((3,)), dma,
            dma((NCH, nz)), dma((NCH, nz)), dma((NCH, nz)), dma((NCH, nz)),
            dma((NCH,)), dma((NCH,)), dma((NCH,)), dma((NCH,)),
            dma((back,)), dma((back,)), dma((n_dev,)), dma((n_dev,)), dma((n_dev,)), dma((n_dev,)),
        ],
        compiler_params=pltpu.CompilerParams(
            collective_id=0, has_side_effects=True, vmem_limit_bytes=63 * 1024 * 1024
        ),
        cost_estimate=pl.CostEstimate(
            flops=2 * rows * width * 768, bytes_accessed=4 * 1024 * 1024, transcendentals=0
        ),
    )(
        hidden, norm_gain[None, :], w_qkv, doc_ids[None, :], target[None, :], freq_row
    )


def solution(mesh):
    in_specs = (
        P(("section", "ctx"), None),
        P(),
        P("ctx", None),
        P(("section", "ctx")),
        P(("section", "ctx")),
    )
    out_specs = P(("section", "ctx"), None)
    return jax.shard_map(body, mesh=mesh, in_specs=in_specs, out_specs=out_specs, check_vma=False)
```

time: 125 us -> 85.1 us (0.68)
  blocking collectives: 41.6 us -> 0 us
  Pallas kernels: 63.4 us -> 81.9 us
  starting transfers between devices: 12.4 us -> 0 us
  local copies, waits for them, and re-layouts: 4.85 us -> 2.92 us
  other arithmetic: 1.72 us -> 0 us
    all_gather x1 -> x0, blocking collectives: 41.6 us -> none  [body(): table = lax.all_gather(target, 'ctx', axis=0, tiled=False)]
    pallas_call x1, Pallas kernels: 63.4 us -> 81.9 us  [body(): pl.pallas_call(functools.partial(kernel, n_dev), out_shape=jax.ShapeDtype...]
    all_to_all x1 -> x0, starting transfers between devices: 12.4 us -> none  [body(): lax.all_to_all(packed.reshape(n_dev, cap, QH * HD), 'ctx', split_axis=0,...]
    unnamed x6 -> x1, local copies, waits for them, and re-layouts: 2.59 us -> 1.57 us
  transfers between devices with their start and end apart: 1 -> 0, of which waited for: 0 -> 0; matrix products, arithmetic and copies ran while one was open for 1% -> 0% of each run, Pallas kernels for 0% -> 0%
where the time goes in v2:
time: 85.1 us; the launch traced here: 84.8 us
  Pallas kernels  81.9 us (96%)
  local copies, waits for them, and re-layouts  2.92 us (3%)
    pallas_call x1, Pallas kernels, body(): pl.pallas_call(functools.partial(kernel, n_dev), out_shape=jax.ShapeDtype...  81.9 us

profile of v2, /device:TPU:0, one launch (start us, length us, event | category | flops | bytes accessed | tf_op | source)
XLA Modules:
  0.0 84.8 jit_solution(9866337139985718789)
XLA Ops:
  0.0 1.3 %broadcast_in_dim.9.gain_ref = bf16[1,8192]{1,0:T(2,128)(2,1)} reshape(bf16[8192]{0:T(1024)(128)(2,1)} %param.7) | data formatting | bytes 32768 | tf_op jit(solution)/shard_map/broadcast_in_dim | solution.py:364
  1.4 81.9 %shard_map.64 = bf16[128,512]{1,0:T(8,128)(2,1)} custom-call(bf16[128,8192]{1,0:T(8,128)(2,1)} %hidden_hbm.1, bf16[1,8192]{1,0:T(2,128)(2,1)} %broadcast_in_dim.9.gain_ref, bf16[256,768]{1,0:T(8,128)(2,1)} %w_hbm.1, s32[1,128]{1,0:T(1,128)} %bitcast.2, s32[1,128]{1,0:T(1,128)} %bitcast.3, f32[1,128]{1,0:T(1,128)} %constant.2.clone.freq_ref), custom_call_target="tpu_custom_call" | custom-call | flops 1610612736 | bytes 4194304 | tf_op jit(solution)/shard_map/pallas_call | solution.py:328
  83.2 1.6 %copy.8 = bf16[128,512]{1,0:T(8,128)(2,1)} copy(bf16[128,512]{1,0:T(8,128)(2,1)} %shard_map.64) | data formatting | bytes 262144

commit v3 on v2

--- a/solution.py
+++ b/solution.py
@@ -84,13 +84,35 @@
     c_dev = z * 8 + y * 4 + x * 2 + (1 - c)
     x_dev = z * 8 + y * 4 + (1 - x) * 2 + c
 
-    def y_copy(n, dz):
-        j = lax.rem(z - dz + nz, nz) * 2 + y
-        return remote(slot(n, j), slot(n, j), y_send.at[n, dz], y_recv.at[n, dz], y_dev)
-
-    def z_copy(n, dz):
-        dev = lax.rem(z + dz, nz) * 8 + y * 4 + x * 2 + c
-        return remote(slot(n, shard), slot(n, shard), z_send.at[n, dz], z_recv.at[n, dz], dev)
+    def y_copy(n, zs):
+        j = zs * 2 + y
+        return remote(slot(n, j), slot(n, j), y_send.at[n, zs], y_recv.at[n, zs], y_dev)
+
+    def z_copy(n, zs, way):
+        j = zs * 2 + y
+        send = z_send.at[n, zs, (way + 1) // 2]
+        return remote(slot(n, j), slot(n, j), send, z_recv.at[n, zs], me + 8 * way)
+
+    def z_own(n):
+        pl.when(z < nz - 1)(lambda: z_copy(n, z, 1).start())
+        pl.when(z > 0)(lambda: z_copy(n, z, -1).start())
+
+    def pass_on(n, k, way):
+        zs = z - k * way
+        last = z == (nz - 1 if way > 0 else 0)
+
+        @pl.when((zs >= 0) & (zs < nz))
+        def _():
+            z_copy(n, zs, way).wait_recv()
+            pl.when(jnp.logical_not(last))(lambda: z_copy(n, zs, way).start())
+            y_copy(n, zs).start()
+
+    def z_left(n, k, way):
+        zs = z - k * way
+        last = z == (nz - 1 if way > 0 else 0)
+        pl.when((zs >= 0) & (zs < nz) & jnp.logical_not(last))(
+            lambda: z_copy(n, zs, way).wait_send()
+        )
 
     def i_copy(d):
         return remote(ids.at[me], ids.at[me], i_send.at[d], i_recv.at[d], lax.rem(me + d, n_dev))
@@ -122,12 +144,9 @@
 
     for n in range(NCH):
         w_load(n).wait()
-        for dz in range(nz):
-            if dz:
-                z_copy(n, dz).start()
-            else:
-                y_copy(n, 0).start()
         if n == 0:
+            z_own(n)
+            y_copy(n, z).start()
             each_other(lambda d: i_copy(d).start())
     load.wait()
 
@@ -165,9 +184,13 @@
     own.start()
 
     def forward(n):
-        for dz in range(1, nz):
-            z_copy(n, dz).wait_recv()
-            y_copy(n, dz).start()
+        for k in range(1, nz):
+            for way in (1, -1):
+                pass_on(n, k, way)
+            if k == 1 and n + 1 < NCH:
+                z_own(n + 1)
+        if n + 1 < NCH:
+            y_copy(n + 1, z).start()
 
     def matmul(n):
         for dz in range(nz):
@@ -228,6 +251,7 @@
     )
 
     forward(1)
+    forward(2)
     own.wait()
     for k in range(3):
         h_copy(k).wait_recv()
@@ -236,12 +260,11 @@
     matmul(1)
     c_copy(1).start()
     cross(0)
-    cross(1)
-    forward(2)
     kv = finish(0)
     kvbuf[back, :, :HD] = rotate(kv[:, :HD], cosine, sine).astype(jnp.bfloat16)
     kvbuf[back, :, HD:] = kv[:, HD:].astype(jnp.bfloat16)
     each_later(lambda d: kv_copy(d).start())
+    cross(1)
     matmul(2)
     c_copy(2).start()
     heads = finish(1)
@@ -307,8 +330,8 @@
         h_copy(k).wait_send()
     for n in range(NCH):
         for dz in range(nz):
-            if dz:
-                z_copy(n, dz).wait_send()
+            for way in (1, -1):
+                z_left(n, dz, way)
             y_copy(n, dz).wait_send()
         c_copy(n).wait_send()
         x_copy(n).wait_send()
@@ -350,7 +373,7 @@
             pltpu.VMEM((n_dev, 2 * cap, QH * HD // 2), bf16),
             dma, dma((NCH,)),
             dma((3,)), dma((3,)), dma,
-            dma((NCH, nz)), dma((NCH, nz)), dma((NCH, nz)), dma((NCH, nz)),
+            dma((NCH, nz, 2)), dma((NCH, nz)), dma((NCH, nz)), dma((NCH, nz)),
             dma((NCH,)), dma((NCH,)), dma((NCH,)), dma((NCH,)),
             dma((back,)), dma((back,)), dma((n_dev,)), dma((n_dev,)), dma((n_dev,)), dma((n_dev,)),
         ],

time: 85.1 us -> 75 us (0.88)
  Pallas kernels: 81.9 us -> 71.7 us
    pallas_call x1, Pallas kernels: 81.9 us -> 71.7 us  [body(): pl.pallas_call(functools.partial(kernel, n_dev), out_shape=jax.ShapeDtype...]
where the time goes in v3:
time: 75 us; the launch traced here: 74.6 us
  Pallas kernels  71.7 us (96%)
  local copies, waits for them, and re-layouts  2.92 us (4%)
    pallas_call x1, Pallas kernels, body(): pl.pallas_call(functools.partial(kernel, n_dev), out_shape=jax.ShapeDtype...  71.7 us
    unnamed x1, local copies, waits for them, and re-layouts  1.57 us

profile of v3, /device:TPU:0, one launch (start us, length us, event | category | flops | bytes accessed | tf_op | source)
XLA Modules:
  0.0 74.6 jit_solution(3802524890635502312)
XLA Ops:
  0.0 1.3 %broadcast_in_dim.9.gain_ref = bf16[1,8192]{1,0:T(2,128)(2,1)} reshape(bf16[8192]{0:T(1024)(128)(2,1)} %param.7) | data formatting | bytes 32768 | tf_op jit(solution)/shard_map/broadcast_in_dim | solution.py:387
  1.4 71.7 %shard_map.64 = bf16[128,512]{1,0:T(8,128)(2,1)} custom-call(bf16[128,8192]{1,0:T(8,128)(2,1)} %hidden_hbm.1, bf16[1,8192]{1,0:T(2,128)(2,1)} %broadcast_in_dim.9.gain_ref, bf16[256,768]{1,0:T(8,128)(2,1)} %w_hbm.1, s32[1,128]{1,0:T(1,128)} %bitcast.2, s32[1,128]{1,0:T(1,128)} %bitcast.3, f32[1,128]{1,0:T(1,128)} %constant.2.clone.freq_ref), custom_call_target="tpu_custom_call" | custom-call | flops 1610612736 | bytes 4194304 | tf_op jit(solution)/shard_map/pallas_call | solution.py:351
  73.0 1.6 %copy.8 = bf16[128,512]{1,0:T(8,128)(2,1)} copy(bf16[128,512]{1,0:T(8,128)(2,1)} %shard_map.64) | data formatting | bytes 262144

commit v4 on v3

--- a/solution.py
+++ b/solution.py
@@ -167,19 +167,21 @@
             ).astype(jnp.bfloat16)
         return carry
 
-    lax.fori_loop(0, rows // step, norm_rows, 0)
-
-    def h_copy(k):
+
+    def h_copy(i):
+        k, part_at = i % 3, pl.ds((i // 3) * (rows // 2), rows // 2)
         dx, dc = ((1, 0), (1, 1), (0, 1))[k]
         ox = 1 - x if dx else x
         oc = 1 - c if dc else c
         return remote(
-            nsend.at[2 * oc + ox], xg.at[spot], h_send.at[k], h_recv.at[k],
+            nsend.at[2 * oc + ox, part_at], xg.at[spot, part_at], h_send.at[i], h_recv.at[i],
             z * 8 + y * 4 + ox * 2 + oc,
         )
 
-    for k in range(3):
-        h_copy(k).start()
+    for i in range(2):
+        lax.fori_loop(i * rows // step // 2, (i + 1) * rows // step // 2, norm_rows, 0)
+        for k in range(3):
+            h_copy(3 * i + k).start()
     own = pltpu.make_async_copy(nsend.at[spot], xg.at[spot], h_own)
     own.start()
 
@@ -231,6 +233,8 @@
         outbuf[:, head * HD : (head + 1) * HD] = (out / total).astype(jnp.bfloat16)
 
     forward(0)
+    forward(1)
+    forward(2)
     each_other(lambda d: i_copy(d).wait_recv())
     doc_col = jnp.transpose(jnp.broadcast_to(doc, (rows, rows)))
     count = jnp.zeros((rows, 1), jnp.float32)
@@ -250,21 +254,19 @@
         lax.broadcasted_iota(jnp.int32, (rows, HD), 1) < HD // 2, -1.0, 1.0
     )
 
-    forward(1)
-    forward(2)
     own.wait()
-    for k in range(3):
+    for k in range(6):
         h_copy(k).wait_recv()
     matmul(0)
     c_copy(0).start()
     matmul(1)
     c_copy(1).start()
     cross(0)
+    cross(1)
     kv = finish(0)
     kvbuf[back, :, :HD] = rotate(kv[:, :HD], cosine, sine).astype(jnp.bfloat16)
     kvbuf[back, :, HD:] = kv[:, HD:].astype(jnp.bfloat16)
     each_later(lambda d: kv_copy(d).start())
-    cross(1)
     matmul(2)
     c_copy(2).start()
     heads = finish(1)
@@ -326,7 +328,7 @@
     each_other(lambda d: i_copy(d).wait_send())
     each_other(lambda d: a_copy(d).wait_send())
     each_later(lambda d: kv_copy(d).wait_send())
-    for k in range(3):
+    for k in range(6):
         h_copy(k).wait_send()
     for n in range(NCH):
         for dz in range(nz):
@@ -372,7 +374,7 @@
             pltpu.VMEM((n_dev, 2 * cap, QH * HD // 2), bf16),
             pltpu.VMEM((n_dev, 2 * cap, QH * HD // 2), bf16),
             dma, dma((NCH,)),
-            dma((3,)), dma((3,)), dma,
+            dma((6,)), dma((6,)), dma,
             dma((NCH, nz, 2)), dma((NCH, nz)), dma((NCH, nz)), dma((NCH, nz)),
             dma((NCH,)), dma((NCH,)), dma((NCH,)), dma((NCH,)),
             dma((back,)), dma((back,)), dma((n_dev,)), dma((n_dev,)), dma((n_dev,)), dma((n_dev,)),

time: 75 us -> 74.8 us (level)
  no operation moved by 1% of the time
where the time goes in v4:
time: 74.8 us; the launch traced here: 74.4 us
  Pallas kernels  71.5 us (96%)
  local copies, waits for them, and re-layouts  2.92 us (4%)
    pallas_call x1, Pallas kernels, body(): pl.pallas_call(functools.partial(kernel, n_dev), out_shape=jax.ShapeDtype...  71.5 us
    unnamed x1, local copies, waits for them, and re-layouts  1.57 us

profile of v4, /device:TPU:0, one launch (start us, length us, event | category | flops | bytes accessed | tf_op | source)
XLA Modules:
  0.0 74.4 jit_solution(1839648789573358433)
XLA Ops:
  0.0 1.3 %broadcast_in_dim.9.gain_ref = bf16[1,8192]{1,0:T(2,128)(2,1)} reshape(bf16[8192]{0:T(1024)(128)(2,1)} %param.7) | data formatting | bytes 32768 | tf_op jit(solution)/shard_map/broadcast_in_dim | solution.py:389
  1.4 71.5 %shard_map.64 = bf16[128,512]{1,0:T(8,128)(2,1)} custom-call(bf16[128,8192]{1,0:T(8,128)(2,1)} %hidden_hbm.1, bf16[1,8192]{1,0:T(2,128)(2,1)} %broadcast_in_dim.9.gain_ref, bf16[256,768]{1,0:T(8,128)(2,1)} %w_hbm.1, s32[1,128]{1,0:T(1,128)} %bitcast.2, s32[1,128]{1,0:T(1,128)} %bitcast.3, f32[1,128]{1,0:T(1,128)} %constant.2.clone.freq_ref), custom_call_target="tpu_custom_call" | custom-call | flops 1610612736 | bytes 4194304 | tf_op jit(solution)/shard_map/pallas_call | solution.py:353
  72.8 1.6 %copy.8 = bf16[128,512]{1,0:T(8,128)(2,1)} copy(bf16[128,512]{1,0:T(8,128)(2,1)} %shard_map.64) | data formatting | bytes 262144
